TPU v7x, 512 devices: a whole 4x4x16 slice. The times are simulated.
512 devices in a mesh: sec: 2 (over core), sp: 4 (over y), dev: 64 (over x, z).
Axes of the slice: x: 4, y: 4, z: 16, core: 2. Of those that a mesh axis runs over, the one named last changes fastest.
Arguments:
- patch_qkv: bfloat16 [65536, 3, 1280], P(('sec', 'sp', 'dev')), may hold values from -13 to 13
- patch_state: bfloat16 [65536, 1280], P(('sec', 'sp', 'dev')), may hold values from -6 to 6
- window_index: int32 [512, 128], P(('sec', 'sp', 'dev')), may hold values from 0 to 127, each once within a row
- patch_owner: int32 [65536, 1], P(('sec', 'sp', 'dev')), may hold values from 0 to 127; in each aligned block of 128 rows (0 to 127, 128 to 255, ...) at most 2 rows name the same one
- source_request: int32 [128, 128], P(('sec', 'dev')), may hold values from 0 to 7, never falling along the last dimension, each value on 1 to 64 neighbouring positions
- norm_gain: float32 [1280], replicated, may hold values from 0.1 to 1.9
- w_qkv: bfloat16 [1280, 3, 1280], P(None, None, 'sp'), may hold values from -0.15625 to 0.15625
- b_qkv: bfloat16 [3, 1280], P(None, 'sp'), may hold values from -12 to 12
Outputs:
- out_rows: bfloat16 [65536, 1280], P(('sec', 'sp', 'dev'))
Inputs may be any that keep to these rules, and one draw needn't show every extreme that they name: `window_index`: each row is a permutation of the 128 local patch indices of one device. `patch_owner`: among the 128 patches of one device no owner is named more than 2 times, and on some device one owner is named exactly 2 times. `source_request`: along each row the request number never falls; each request covers 1 to 64 consecutive source positions, one exactly 64.
All inputs are finite; a program needn't handle non-finite values.
Results may differ from a plain program's by a relative error of at most 0.012.
The roundings to bfloat16 on the way count: a program that leaves them out, or rounds other values in their place, can miss the bound.
Values may be sent and summed in bfloat16 or wider, within the bound.
A program may use at most 64 MiB of HBM per device.

v0:
```python
import jax
import jax.numpy as jnp
from jax import lax
from jax.sharding import PartitionSpec as P

HD = 80
WIN = 64


NORM_EPS = 1e-06


def normalize(rows_in, gain_row):
    rows_in = rows_in.astype(jnp.float32)
    mean_sq = jnp.mean(rows_in * rows_in, axis=-1, keepdims=True)
    return (rows_in * lax.rsqrt(mean_sq + NORM_EPS) * gain_row).astype(jnp.bfloat16)


def softmax_rows(scores):
    row_max = jnp.max(scores, axis=-1, keepdims=True)
    expo_vals = jnp.exp(scores - row_max)
    return (expo_vals / jnp.sum(expo_vals, axis=-1, keepdims=True)).astype(jnp.bfloat16)


def window_attend(qkv_rows, order_ids, head_size, window_span):
    num_rows = qkv_rows.shape[0]
    row_width = qkv_rows.shape[2]
    head_count = row_width // head_size
    ordered = jnp.take(qkv_rows, order_ids, axis=0)
    ordered = ordered.reshape(num_rows // window_span, window_span, 3, head_count, head_size)
    scores = jnp.einsum(
        "wqhd,wkhd->whqk", ordered[:, :, 0], ordered[:, :, 1], preferred_element_type=jnp.float32
    ) * head_size ** (-0.5)
    weights = softmax_rows(scores)
    mixed = jnp.einsum(
        "whqk,wkhd->wqhd", weights, ordered[:, :, 2], preferred_element_type=jnp.float32
    )
    mixed = mixed.reshape(num_rows, row_width).astype(jnp.bfloat16)
    return jnp.zeros((num_rows, row_width), jnp.bfloat16).at[order_ids].set(mixed)


def owner_attend(query, keys_all, values_all, request, live_keys, head_size):
    group_size, head_count, _ = query.shape
    q_block = 512
    scale = head_size ** (-0.5)
    open_keys = live_keys > 0

    def one_block(block_start):
        rows_q = lax.dynamic_slice_in_dim(query, block_start, q_block, 0)
        reqs_q = lax.dynamic_slice_in_dim(request, block_start, q_block, 0)
        scores = jnp.einsum("qhd,khd->hqk", rows_q, keys_all, preferred_element_type=jnp.float32)
        allowed = (reqs_q[:, None] == request[None, :]) & open_keys[None, :]
        scores = jnp.where(allowed[None], scores * scale, -1e30)
        weights = softmax_rows(scores)
        mixed = jnp.einsum("hqk,khd->qhd", weights, values_all, preferred_element_type=jnp.float32)
        return mixed.astype(jnp.bfloat16)

    starts = jnp.arange(group_size // q_block, dtype=jnp.int32) * q_block
    blocks = lax.map(one_block, starts)
    return blocks.reshape(group_size, head_count * head_size)


def shards(
    patch_qkv, patch_state, window_index, patch_owner, source_request, norm_gain, w_qkv, b_qkv
):
    num_rows = patch_qkv.shape[0]
    row_width = patch_qkv.shape[2]
    sections = lax.axis_size("sec")
    groups = lax.axis_size("sp")
    members = lax.axis_size("dev")
    owners = sections * members
    capacity = max(2, 2 * num_rows // owners)
    local_width = w_qkv.shape[2]
    local_heads = local_width // HD
    window_out = lax.optimization_barrier(window_attend(patch_qkv, window_index[0], HD, WIN))
    moved = (patch_state.astype(jnp.float32) + window_out.astype(jnp.float32)).astype(jnp.bfloat16)
    owner_id = patch_owner[:, 0]
    owner_hits = (owner_id[:, None] == jnp.arange(owners, dtype=jnp.int32)[None, :]).astype(
        jnp.int32
    )
    slot_rank = jnp.sum((jnp.cumsum(owner_hits, axis=0) - 1) * owner_hits, axis=1)
    slot_id = owner_id * capacity + slot_rank
    picker = (jnp.arange(owners * capacity, dtype=jnp.int32)[:, None] == slot_id[None, :]).astype(
        jnp.bfloat16
    )
    outgoing = jnp.dot(picker, moved, preferred_element_type=jnp.float32).astype(jnp.bfloat16)
    outgoing = outgoing.reshape(owners, capacity, row_width)
    filled = jnp.max(picker, axis=1).reshape(owners, capacity)
    incoming, arrived = (
        lax.all_to_all(outgoing, ("sec", "dev"), split_axis=0, concat_axis=0, tiled=True),
        lax.all_to_all(filled, ("sec", "dev"), split_axis=0, concat_axis=0, tiled=True),
    )
    group_size = owners * groups * capacity
    rows_all, live_all = (
        lax.all_gather(incoming, "sp", axis=1, tiled=True),
        lax.all_gather(arrived, "sp", axis=1, tiled=True),
    )
    normed = normalize(rows_all.reshape(group_size, row_width), norm_gain)
    projected = jnp.einsum("gf,fch->gch", normed, w_qkv, preferred_element_type=jnp.float32)
    projected = (projected + b_qkv.astype(jnp.float32)).astype(jnp.bfloat16)
    query = projected[:, 0].reshape(group_size, local_heads, HD)
    keys_all = projected[:, 1].reshape(group_size, local_heads, HD)
    values_all = projected[:, 2].reshape(group_size, local_heads, HD)
    request = jnp.repeat(source_request[0], groups * capacity)
    live_keys = live_all.reshape(group_size)
    mixed = owner_attend(query, keys_all, values_all, request, live_keys, HD)
    pieces = mixed.reshape(owners, groups, capacity, local_width)
    returned = lax.all_to_all(pieces, "sp", split_axis=1, concat_axis=3, tiled=True).reshape(
        owners, capacity, row_width
    )
    result = lax.all_to_all(returned, ("sec", "dev"), split_axis=0, concat_axis=0, tiled=True)
    result = result.reshape(owners * capacity, row_width)
    back_rows = jnp.einsum("sp,sw->pw", picker, result, preferred_element_type=jnp.float32)
    return (moved.astype(jnp.float32) + back_rows).astype(jnp.bfloat16)


def solution(mesh):
    in_specs = (
        P(("sec", "sp", "dev"), None, None),
        P(("sec", "sp", "dev"), None),
        P(("sec", "sp", "dev"), None),
        P(("sec", "sp", "dev"), None),
        P(("sec", "dev"), None),
        P(),
        P(None, None, "sp"),
        P(None, "sp"),
    )
    out_specs = P(("sec", "sp", "dev"), None)
    return jax.shard_map(shards, mesh=mesh, in_specs=in_specs, out_specs=out_specs, check_vma=False)
```

profile of v0, /device:TPU:1, one launch (start us, length us, event | category | flops | bytes accessed | tf_op | source)
XLA Modules:
  0.0 257.2 jit_solution(1975746845730645650)
XLA Ops:
  7.4 3.8 %gather_fusion = bf16[128,3,1280]{2,0,1:T(8,128)(2,1)S(1)} fusion(bf16[128,3,1280]{2,0,1:T(8,128)(2,1)} %param.10, s32[1024]{0:T(1024)S(1)} %pad_clamp_fusion), kind=kCustom, calls=%fused_computation | custom fusion | bytes 1966592 | tf_op jit(solution)/shard_map/jit(_take)/gather | solution.py:29
  11.2 3.3 %gather.7 = bf16[2,64,3,16,80]{4,3,1,0,2:T(8,128)(2,1)} reshape(bf16[128,3,1280]{2,0,1:T(8,128)(2,1)S(1)} %gather_fusion) | data formatting | bytes 1966080 | tf_op jit(solution)/shard_map/jit(_take)/gather | solution.py:29
  15.7 1.8 copy_select_fusion
  18.7 1.4 convolution_multiply_fusion
  20.0 1.7 fusion.60
  21.8 3.0 %fusion.42 = bf16[2,64,16,80]{3,1,2,0:T(8,128)(2,1)} fusion(bf16[2,64,3,16,80]{4,1,3,0,2:T(8,128)(2,1)} %copy-done.1, f32[2,16,64]{2,1,0:T(8,128)S(1)} %fusion.60, f32[2,16,64,64]{2,3,1,0:T(8,128)} %convolution_multiply_fusion), kind=kOutput, calls=%fused_computation.45 | convolution fusion | flops 21530688 | bytes 1843200 | tf_op jit(solution)/shard_map/whqk,wkhd->wqhd/dot_general | solution.py:35
  24.8 1.4 copy.58
  26.1 1.3 reshape.157
  27.4 1.7 scatter_custom_fusion
  29.6 1.2 convolution_convert_fusion
  30.7 2.0 reshape.141
  32.8 55.9 %all_to_all.38 = bf16[128,2,1280]{2,1,0:T(2,128)(2,1)S(1)} all-to-all(bf16[128,2,1280]{2,1,0:T(2,128)(2,1)S(1)} %reshape.141), channel_id=1, replica_groups=mesh['sec'=2,'sp'=4,'dev'=64] {'sec','dev'}, dimensions={0} | all-to-all | bytes 1310720 | tf_op jit(solution)/shard_map/all_to_all | solution.py:90
  90.5 10.6 %all-to-all-start = ((bf16[128,1,2]{2,1,0:T(2,128)(2,1)}), bf16[128,1,2]{2,1,0:T(2,128)(2,1)S(1)}, u32[]{:S(2)}, u32[]{:S(2)}) async-start(bf16[128,1,2]{2,1,0:T(2,128)(2,1)} %all_to_all.33), calls=%async_computation | async-start | bytes 131072 | tf_op jit(solution)/shard_map/all_to_all | solution.py:91
  101.3 14.4 %all-to-all-done = bf16[128,1,2]{2,1,0:T(2,128)(2,1)S(1)} async-done(((bf16[128,1,2]{2,1,0:T(2,128)(2,1)}), bf16[128,1,2]{2,1,0:T(2,128)(2,1)S(1)}, u32[]{:S(2)}, u32[]{:S(2)}) %all-to-all-start) | async-done | bytes 544 | tf_op jit(solution)/shard_map/all_to_all | solution.py:91
  115.9 9.0 %all-gather = bf16[128,1,8]{0,1,2:T(2,128)(2,1)S(1)} all-gather(bf16[128,1,2]{0,1,2:T(2,128)(2,1)S(1)} %copy.60), channel_id=2, replica_groups=mesh['sec'=2,'sp'=4,'dev'=64] {'sp'}, dimensions={2}, use_global_device_ids=true | all-gather | bytes 2560 | tf_op jit(solution)/shard_map/all_gather | solution.py:96
  125.1 2.8 %all-gather.3.cloned.1.call-done = bf16[128,8,1280]{2,0,1:T(8,128)(2,1)} async-done(((bf16[128,2,1280]{2,0,1:T(8,128)(2,1)}), bf16[128,8,1280]{2,0,1:T(8,128)(2,1)}) %all-gather.3.cloned.1.call-update) | async-done | bytes 2621456 | tf_op jit(solution)/shard_map/all_gather | solution.py:95
  127.9 3.2 %fusion.30 = f32[128,8]{1,0:T(8,128)S(1)} fusion(bf16[128,8,1280]{2,0,1:T(8,128)(2,1)} %all-gather.3.cloned.1.call-done), kind=kLoop, calls=%fused_computation.30 | loop fusion | flops 3931136 | bytes 2625536 | tf_op jit(solution)/shard_map/reduce_sum | solution.py:15
  131.2 5.0 %add_convert_fusion = bf16[1024,3,320]{0,2,1:T(8,128)(2,1)S(1)} fusion(f32[3,320]{1,0:T(4,128)S(1)} %convert_element_type.78, bf16[1280,3,320]{0,2,1:T(8,128)(2,1)S(1)} %copy-done, f32[1280]{0:T(1024)S(1)} %copy-done.8, f32[1024]{0:T(1024)S(1)} %rsqrt.12, bf16[128,8,1280]{2,0,1:T(8,128)(2,1)} %all-gather.3.cloned.1.call-done), kind=kOutput, calls=%fused_computation.31 | convolution fusion | flops 2523791360 | bytes 7058176 | tf_op jit(solution)/shard_map/gf,fch->gch/dot_general | solution.py:99
  136.2 1.4 fusion.59
  137.5 33.7 %while.11 = (s32[]{:T(128)}, bf16[2,512,4,80]{1,3,2,0:T(8,128)(2,1)}, s32[2]{0:T(128)S(1)}, s32[1024]{0:T(1024)S(1)}, pred[1024]{0:T(1024)(128)(4,1)S(1)}, /*ind...) while((s32[]{:T(128)}, ...), condition=%wide.region_10.11_spmd.clone, body=%wide.region_7.10_spmd.clone.sunk | while | flops 684884992 | bytes 19833004 | solution.py:59
  141.0 7.8 %fusion.75 = (f32[4,512]{1,0:T(4,128)S(1)}, f32[4,512,1024]{2,1,0:T(8,128)}) fusion(pred[512,1024]{1,0:T(8,128)(4,1)S(1)} %compare_and_fusion.3, bf16[1024,4,80]{0,2,1:T(8,128)(2,1)} %get-tuple-element.186, bf16[1024,4,80]{0,2,1:T(8,128)(2,1)} %get-tuple-element.185, s32[]{:T(128)S(6)} %select_n.56), kind=kOutput, calls=%fused_computation.73.clone.1 | convolution fusion | flops 343933952 | bytes 9904132 | tf_op jit(solution)/shard_map/while/body/eval_jaxpr/sub | solution.py:21
  148.7 5.7 %fusion.76 = bf16[2,512,4,80]{1,3,2,0:T(8,128)(2,1)} fusion(bf16[2,512,4,80]{1,3,2,0:T(8,128)(2,1)} %get-tuple-element.169, s32[]{:T(128)} %get-tuple-element.168, bf16[1024,4,80]{0,2,1:T(8,128)(2,1)} %get-tuple-element.187, f32[4,512,1024]{2,1,0:T(8,128)} %get-tuple-element.154, f32[4,512]{1,0:T(4,128)S(1)} %get-tuple-element.155), kind=kOutput, calls=%fused_computation.15.clone.1 | convolution fusion | flops 339902464 | bytes 9380352 | tf_op jit(solution)/shard_map/while/body/eval_jaxpr/hqk,khd->qhd/dot_general | solution.py:55
  157.8 7.7 %fusion.75 = (f32[4,512]{1,0:T(4,128)S(1)}, f32[4,512,1024]{2,1,0:T(8,128)}) fusion(pred[512,1024]{1,0:T(8,128)(4,1)S(1)} %compare_and_fusion.3, bf16[1024,4,80]{0,2,1:T(8,128)(2,1)} %get-tuple-element.186, bf16[1024,4,80]{0,2,1:T(8,128)(2,1)} %get-tuple-element.185, s32[]{:T(128)S(6)} %select_n.56), kind=kOutput, calls=%fused_computation.73.clone.1 | convolution fusion | flops 343933952 | bytes 9904132 | tf_op jit(solution)/shard_map/while/body/eval_jaxpr/sub | solution.py:21
  165.6 5.7 %fusion.76 = bf16[2,512,4,80]{1,3,2,0:T(8,128)(2,1)} fusion(bf16[2,512,4,80]{1,3,2,0:T(8,128)(2,1)} %get-tuple-element.169, s32[]{:T(128)} %get-tuple-element.168, bf16[1024,4,80]{0,2,1:T(8,128)(2,1)} %get-tuple-element.187, f32[4,512,1024]{2,1,0:T(8,128)} %get-tuple-element.154, f32[4,512]{1,0:T(4,128)S(1)} %get-tuple-element.155), kind=kOutput, calls=%fused_computation.15.clone.1 | convolution fusion | flops 339902464 | bytes 9380352 | tf_op jit(solution)/shard_map/while/body/eval_jaxpr/hqk,khd->qhd/dot_general | solution.py:55
  171.3 1.6 copy.64
  172.9 2.8 %reshape_reshape.3 = bf16[128,4,2,320]{3,2,1,0:T(2,128)(2,1)} reshape(bf16[2,512,4,80]{3,2,1,0:T(4,128)(2,1)S(1)} %copy.64) | data formatting | bytes 1310720 | tf_op jit(solution)/shard_map/reshape;reshape | solution.py:107
  175.7 2.4 copy.65
  178.1 12.6 %all_to_all.39 = bf16[128,4,2,320]{0,3,2,1:T(8,128)(2,1)S(1)} all-to-all(bf16[128,4,2,320]{0,3,2,1:T(8,128)(2,1)S(1)} %copy.65), channel_id=1, replica_groups=mesh['sec'=2,'sp'=4,'dev'=64] {'sp'}, dimensions={1} | all-to-all | bytes 1310720 | tf_op jit(solution)/shard_map/all_to_all | solution.py:108
  190.7 1.9 copy.67
  192.6 53.6 %all_to_all.40 = bf16[128,2,1280]{2,1,0:T(2,128)(2,1)} all-to-all(bf16[128,2,1280]{2,1,0:T(2,128)(2,1)} %copy.67), channel_id=1, replica_groups=mesh['sec'=2,'sp'=4,'dev'=64] {'sec','dev'}, dimensions={0} | all-to-all | bytes 1310720 | tf_op jit(solution)/shard_map/all_to_all | solution.py:111
  246.2 2.1 reshape.143
  248.3 2.0 fusion.36
  (57 shorter events, 8.8 us)
Async XLA Ops:
  6.5 124.7 %copy-start = (bf16[1280,3,320]{0,2,1:T(8,128)(2,1)S(1)}, bf16[1280,3,320]{0,2,1:T(8,128)(2,1)}, u32[]{:S(2)}) copy-start(bf16[1280,3,320]{0,2,1:T(8,128)(2,1)} %param.16) | copy-start | bytes 7372804
  6.5 121.3 %all-gather.3.cloned.1.call-start = ((), (), s32[]{:S(2)}) async-start(), calls=%async_computation.4 | async-start | bytes 3276800 | tf_op jit(solution)/shard_map/all_gather | solution.py:95
  7.4 7.6 %copy-start.9 = (s32[1,128]{1,0:T(1,128)S(1)}, s32[1,128]{1,0:T(1,128)}, u32[]{:S(2)}) copy-start(s32[1,128]{1,0:T(1,128)} %param.12) | copy-start | bytes 1540
  17.5 1.2 copy-start.1
  21.7 7.4 %copy-start.7 = (s32[128,1]{0,1:T(1,128)S(1)}, s32[128,1]{0,1:T(1,128)}, u32[]{:S(2)}) copy-start(s32[128,1]{0,1:T(1,128)} %param.13) | copy-start | bytes 1540
  21.7 7.8 %copy-start.4 = (bf16[128,1280]{1,0:T(8,128)(2,1)S(1)}, bf16[128,1280]{1,0:T(8,128)(2,1)}, u32[]{:S(2)}) copy-start(bf16[128,1280]{1,0:T(8,128)(2,1)} %param.11) | copy-start | bytes 983044
  29.1 60.5 %copy-start.2 = (bf16[128,1280]{1,0:T(8,128)(2,1)}, bf16[128,1280]{1,0:T(8,128)(2,1)S(1)}, u32[]{:S(2)}) copy-start(bf16[128,1280]{1,0:T(8,128)(2,1)S(1)} %scatter_custom_fusion) | copy-start | bytes 983044
  30.7 70.4 %copy-start.6 = (bf16[3,320]{1,0:T(4,128)(2,1)S(1)}, bf16[3,320]{1,0:T(4,128)(2,1)}, u32[]{:S(2)}) copy-start(bf16[3,320]{1,0:T(4,128)(2,1)} %param.17) | copy-start | bytes 5764
  30.7 70.4 %copy-start.5 = (s32[1,128]{1,0:T(1,128)S(1)}, s32[1,128]{1,0:T(1,128)}, u32[]{:S(2)}) copy-start(s32[1,128]{1,0:T(1,128)} %param.14) | copy-start | bytes 1540
  88.7 42.5 %copy-start.8 = (f32[1280]{0:T(1024)S(1)}, f32[1280]{0:T(1024)}, u32[]{:S(2)}) copy-start(f32[1280]{0:T(1024)} %param.15) | copy-start | bytes 15364
  90.5 25.3 %all-to-all-start = ((bf16[128,1,2]{2,1,0:T(2,128)(2,1)}), bf16[128,1,2]{2,1,0:T(2,128)(2,1)S(1)}, u32[]{:S(2)}, u32[]{:S(2)}) async-start(bf16[128,1,2]{2,1,0:T(2,128)(2,1)} %all_to_all.33), calls=%async_computation | async-start | bytes 131072 | tf_op jit(solution)/shard_map/all_to_all | solution.py:91
  190.6 57.6 %copy-start.3 = (bf16[128,1280]{1,0:T(8,128)(2,1)S(1)}, bf16[128,1280]{1,0:T(8,128)(2,1)}, u32[]{:S(2)}) copy-start(bf16[128,1280]{1,0:T(8,128)(2,1)} %copy-done.2) | copy-start | bytes 983044
Sparse Core Ops, SparseCore 0:
  89.7 38.1 all-gather.2
where the time goes:
time: 259 us; the launch traced here: 257 us
  blocking collectives  131 us (51%)
  matrix products  41.1 us (16%)
  local copies, waits for them, and re-layouts  31.6 us (12%)
  waiting for transfers between devices  17.3 us (7%)
  between operations  13.6 us (5%)
  starting transfers between devices  10.6 us (4%)
  other arithmetic  7.85 us (3%)
  loops' own time  4.18 us (2%)
    all_to_all x1, blocking collectives, shards(): lax.all_to_all(outgoing, ('sec', 'dev'), split_axis=0, concat_axis=0, til...  55.9 us
    all_to_all x1, blocking collectives, shards(): lax.all_to_all(returned, ('sec', 'dev'), split_axis=0, concat_axis=0, til...  53.6 us
    sub x3, matrix products, softmax_rows(): expo_vals = jnp.exp(scores - row_max)  17.2 us
    all_to_all x1, waiting for transfers between devices, shards(): lax.all_to_all(filled, ('sec', 'dev'), split_axis=0, concat_axis=0, tiled...  14.4 us
    all_to_all x1, blocking collectives, shards(): lax.all_to_all(pieces, 'sp', split_axis=1, concat_axis=3, tiled=True)  12.6 us
    dot_general x2, matrix products, one_block(): jnp.einsum('hqk,khd->qhd', weights, values_all, preferred_element_type=jn...  11.4 us
    all_to_all x1, starting transfers between devices, shards(): lax.all_to_all(filled, ('sec', 'dev'), split_axis=0, concat_axis=0, tiled...  10.6 us
    all_gather x1, blocking collectives, shards(): lax.all_gather(arrived, 'sp', axis=1, tiled=True)  8.95 us
  transfers between devices with their start and end apart: 2, of which 2 were waited for; matrix products, arithmetic and copies ran while one was open for 0% of the time, Pallas kernels for 0%

commit v1 on v0

--- a/solution.py
+++ b/solution.py
@@ -75,10 +75,9 @@
     window_out = lax.optimization_barrier(window_attend(patch_qkv, window_index[0], HD, WIN))
     moved = (patch_state.astype(jnp.float32) + window_out.astype(jnp.float32)).astype(jnp.bfloat16)
     owner_id = patch_owner[:, 0]
-    owner_hits = (owner_id[:, None] == jnp.arange(owners, dtype=jnp.int32)[None, :]).astype(
-        jnp.int32
-    )
-    slot_rank = jnp.sum((jnp.cumsum(owner_hits, axis=0) - 1) * owner_hits, axis=1)
+    position = jnp.arange(num_rows, dtype=jnp.int32)
+    earlier = (owner_id[:, None] == owner_id[None, :]) & (position[None, :] < position[:, None])
+    slot_rank = jnp.sum(earlier.astype(jnp.int32), axis=1)
     slot_id = owner_id * capacity + slot_rank
     picker = (jnp.arange(owners * capacity, dtype=jnp.int32)[:, None] == slot_id[None, :]).astype(
         jnp.bfloat16

time: 259 us -> 259 us (level)
  no operation moved by 1% of the time
where the time goes in v1:
time: 259 us; the launch traced here: 257 us
  blocking collectives  131 us (51%)
  matrix products  41.1 us (16%)
  local copies, waits for them, and re-layouts  31.6 us (12%)
  waiting for transfers between devices  17.3 us (7%)
  between operations  13.6 us (5%)
  starting transfers between devices  10.6 us (4%)
  other arithmetic  7.6 us (3%)
  loops' own time  4.18 us (2%)
    all_to_all x1, blocking collectives, shards(): lax.all_to_all(outgoing, ('sec', 'dev'), split_axis=0, concat_axis=0, til...  55.9 us
    all_to_all x1, blocking collectives, shards(): lax.all_to_all(returned, ('sec', 'dev'), split_axis=0, concat_axis=0, til...  53.6 us
    sub x3, matrix products, softmax_rows(): expo_vals = jnp.exp(scores - row_max)  17.2 us
    all_to_all x1, waiting for transfers between devices, shards(): lax.all_to_all(filled, ('sec', 'dev'), split_axis=0, concat_axis=0, tiled...  14.4 us
    all_to_all x1, blocking collectives, shards(): lax.all_to_all(pieces, 'sp', split_axis=1, concat_axis=3, tiled=True)  12.6 us
    dot_general x2, matrix products, one_block(): jnp.einsum('hqk,khd->qhd', weights, values_all, preferred_element_type=jn...  11.4 us
    all_to_all x1, starting transfers between devices, shards(): lax.all_to_all(filled, ('sec', 'dev'), split_axis=0, concat_axis=0, tiled...  10.6 us
    all_gather x1, blocking collectives, shards(): lax.all_gather(arrived, 'sp', axis=1, tiled=True)  8.95 us
  transfers between devices with their start and end apart: 2, of which 2 were waited for; matrix products, arithmetic and copies ran while one was open for 0% of the time, Pallas kernels for 0%

profile of v1, /device:TPU:1, one launch (start us, length us, event | category | flops | bytes accessed | tf_op | source)
XLA Modules:
  0.0 256.9 jit_solution(17895793349097895429)
XLA Ops:
  7.4 3.8 %gather_fusion = bf16[128,3,1280]{2,0,1:T(8,128)(2,1)S(1)} fusion(bf16[128,3,1280]{2,0,1:T(8,128)(2,1)} %param.10, s32[1024]{0:T(1024)S(1)} %pad_clamp_fusion), kind=kCustom, calls=%fused_computation | custom fusion | bytes 1966592 | tf_op jit(solution)/shard_map/jit(_take)/gather | solution.py:29
  11.2 3.3 %gather.7 = bf16[2,64,3,16,80]{4,3,1,0,2:T(8,128)(2,1)} reshape(bf16[128,3,1280]{2,0,1:T(8,128)(2,1)S(1)} %gather_fusion) | data formatting | bytes 1966080 | tf_op jit(solution)/shard_map/jit(_take)/gather | solution.py:29
  15.7 1.8 copy_select_fusion
  18.7 1.4 convolution_multiply_fusion
  20.0 1.7 fusion.60
  21.8 3.0 %fusion.42 = bf16[2,64,16,80]{3,1,2,0:T(8,128)(2,1)} fusion(bf16[2,64,3,16,80]{4,1,3,0,2:T(8,128)(2,1)} %copy-done.1, f32[2,16,64]{2,1,0:T(8,128)S(1)} %fusion.60, f32[2,16,64,64]{2,3,1,0:T(8,128)} %convolution_multiply_fusion), kind=kOutput, calls=%fused_computation.45 | convolution fusion | flops 21530688 | bytes 1843200 | tf_op jit(solution)/shard_map/whqk,wkhd->wqhd/dot_general | solution.py:35
  24.8 1.4 copy.58
  26.1 1.3 reshape.158
  27.4 1.7 scatter_custom_fusion
  29.3 1.2 convolution_convert_fusion
  30.5 2.0 reshape.142
  32.5 55.9 %all_to_all.38 = bf16[128,2,1280]{2,1,0:T(2,128)(2,1)S(1)} all-to-all(bf16[128,2,1280]{2,1,0:T(2,128)(2,1)S(1)} %reshape.142), channel_id=1, replica_groups=mesh['sec'=2,'sp'=4,'dev'=64] {'sec','dev'}, dimensions={0} | all-to-all | bytes 1310720 | tf_op jit(solution)/shard_map/all_to_all | solution.py:89
  90.3 10.6 %all-to-all-start = ((bf16[128,1,2]{2,1,0:T(2,128)(2,1)}), bf16[128,1,2]{2,1,0:T(2,128)(2,1)S(1)}, u32[]{:S(2)}, u32[]{:S(2)}) async-start(bf16[128,1,2]{2,1,0:T(2,128)(2,1)} %all_to_all.33), calls=%async_computation | async-start | bytes 131072 | tf_op jit(solution)/shard_map/all_to_all | solution.py:90
  101.1 14.4 %all-to-all-done = bf16[128,1,2]{2,1,0:T(2,128)(2,1)S(1)} async-done(((bf16[128,1,2]{2,1,0:T(2,128)(2,1)}), bf16[128,1,2]{2,1,0:T(2,128)(2,1)S(1)}, u32[]{:S(2)}, u32[]{:S(2)}) %all-to-all-start) | async-done | bytes 544 | tf_op jit(solution)/shard_map/all_to_all | solution.py:90
  115.6 8.9 %all-gather = bf16[128,1,8]{0,1,2:T(2,128)(2,1)S(1)} all-gather(bf16[128,1,2]{0,1,2:T(2,128)(2,1)S(1)} %copy.60), channel_id=2, replica_groups=mesh['sec'=2,'sp'=4,'dev'=64] {'sp'}, dimensions={2}, use_global_device_ids=true | all-gather | bytes 2560 | tf_op jit(solution)/shard_map/all_gather | solution.py:95
  124.8 2.8 %all-gather.3.cloned.1.call-done = bf16[128,8,1280]{2,0,1:T(8,128)(2,1)} async-done(((bf16[128,2,1280]{2,0,1:T(8,128)(2,1)}), bf16[128,8,1280]{2,0,1:T(8,128)(2,1)}) %all-gather.3.cloned.1.call-update) | async-done | bytes 2621456 | tf_op jit(solution)/shard_map/all_gather | solution.py:94
  127.6 3.2 %fusion.30 = f32[128,8]{1,0:T(8,128)S(1)} fusion(bf16[128,8,1280]{2,0,1:T(8,128)(2,1)} %all-gather.3.cloned.1.call-done), kind=kLoop, calls=%fused_computation.30 | loop fusion | flops 3931136 | bytes 2625536 | tf_op jit(solution)/shard_map/reduce_sum | solution.py:15
  130.9 4.9 %add_convert_fusion = bf16[1024,3,320]{0,2,1:T(8,128)(2,1)S(1)} fusion(f32[3,320]{1,0:T(4,128)S(1)} %convert_element_type.78, bf16[1280,3,320]{0,2,1:T(8,128)(2,1)S(1)} %copy-done, f32[1280]{0:T(1024)S(1)} %copy-done.7, f32[1024]{0:T(1024)S(1)} %rsqrt.12, bf16[128,8,1280]{2,0,1:T(8,128)(2,1)} %all-gather.3.cloned.1.call-done), kind=kOutput, calls=%fused_computation.31 | convolution fusion | flops 2523791360 | bytes 7058176 | tf_op jit(solution)/shard_map/gf,fch->gch/dot_general | solution.py:98
  135.9 1.4 fusion.59
  137.3 33.7 %while.11 = (s32[]{:T(128)}, bf16[2,512,4,80]{1,3,2,0:T(8,128)(2,1)}, s32[2]{0:T(128)S(1)}, s32[1024]{0:T(1024)S(1)}, pred[1024]{0:T(1024)(128)(4,1)S(1)}, /*ind...) while((s32[]{:T(128)}, ...), condition=%wide.region_9.10_spmd.clone, body=%wide.region_6.0_spmd.clone.sunk | while | flops 684884992 | bytes 19833004 | solution.py:59
  140.7 7.8 %fusion.75 = (f32[4,512]{1,0:T(4,128)S(1)}, f32[4,512,1024]{2,1,0:T(8,128)}) fusion(pred[512,1024]{1,0:T(8,128)(4,1)S(1)} %compare_and_fusion.3, bf16[1024,4,80]{0,2,1:T(8,128)(2,1)} %get-tuple-element.186, bf16[1024,4,80]{0,2,1:T(8,128)(2,1)} %get-tuple-element.185, s32[]{:T(128)S(6)} %select_n.56), kind=kOutput, calls=%fused_computation.73.clone.1 | convolution fusion | flops 343933952 | bytes 9904132 | tf_op jit(solution)/shard_map/while/body/eval_jaxpr/sub | solution.py:21
  148.5 5.7 %fusion.76 = bf16[2,512,4,80]{1,3,2,0:T(8,128)(2,1)} fusion(bf16[2,512,4,80]{1,3,2,0:T(8,128)(2,1)} %get-tuple-element.169, s32[]{:T(128)} %get-tuple-element.168, bf16[1024,4,80]{0,2,1:T(8,128)(2,1)} %get-tuple-element.187, f32[4,512,1024]{2,1,0:T(8,128)} %get-tuple-element.154, f32[4,512]{1,0:T(4,128)S(1)} %get-tuple-element.155), kind=kOutput, calls=%fused_computation.15.clone.1 | convolution fusion | flops 339902464 | bytes 9380352 | tf_op jit(solution)/shard_map/while/body/eval_jaxpr/hqk,khd->qhd/dot_general | solution.py:55
  157.6 7.7 %fusion.75 = (f32[4,512]{1,0:T(4,128)S(1)}, f32[4,512,1024]{2,1,0:T(8,128)}) fusion(pred[512,1024]{1,0:T(8,128)(4,1)S(1)} %compare_and_fusion.3, bf16[1024,4,80]{0,2,1:T(8,128)(2,1)} %get-tuple-element.186, bf16[1024,4,80]{0,2,1:T(8,128)(2,1)} %get-tuple-element.185, s32[]{:T(128)S(6)} %select_n.56), kind=kOutput, calls=%fused_computation.73.clone.1 | convolution fusion | flops 343933952 | bytes 9904132 | tf_op jit(solution)/shard_map/while/body/eval_jaxpr/sub | solution.py:21
  165.3 5.7 %fusion.76 = bf16[2,512,4,80]{1,3,2,0:T(8,128)(2,1)} fusion(bf16[2,512,4,80]{1,3,2,0:T(8,128)(2,1)} %get-tuple-element.169, s32[]{:T(128)} %get-tuple-element.168, bf16[1024,4,80]{0,2,1:T(8,128)(2,1)} %get-tuple-element.187, f32[4,512,1024]{2,1,0:T(8,128)} %get-tuple-element.154, f32[4,512]{1,0:T(4,128)S(1)} %get-tuple-element.155), kind=kOutput, calls=%fused_computation.15.clone.1 | convolution fusion | flops 339902464 | bytes 9380352 | tf_op jit(solution)/shard_map/while/body/eval_jaxpr/hqk,khd->qhd/dot_general | solution.py:55
  171.0 1.6 copy.64
  172.6 2.8 %reshape_reshape.3 = bf16[128,4,2,320]{3,2,1,0:T(2,128)(2,1)} reshape(bf16[2,512,4,80]{3,2,1,0:T(4,128)(2,1)S(1)} %copy.64) | data formatting | bytes 1310720 | tf_op jit(solution)/shard_map/reshape;reshape | solution.py:106
  175.5 2.4 copy.65
  177.8 12.6 %all_to_all.39 = bf16[128,4,2,320]{0,3,2,1:T(8,128)(2,1)S(1)} all-to-all(bf16[128,4,2,320]{0,3,2,1:T(8,128)(2,1)S(1)} %copy.65), channel_id=1, replica_groups=mesh['sec'=2,'sp'=4,'dev'=64] {'sp'}, dimensions={1} | all-to-all | bytes 1310720 | tf_op jit(solution)/shard_map/all_to_all | solution.py:107
  190.4 1.9 copy.67
  192.3 53.6 %all_to_all.40 = bf16[128,2,1280]{2,1,0:T(2,128)(2,1)} all-to-all(bf16[128,2,1280]{2,1,0:T(2,128)(2,1)} %copy.67), channel_id=1, replica_groups=mesh['sec'=2,'sp'=4,'dev'=64] {'sec','dev'}, dimensions={0} | all-to-all | bytes 1310720 | tf_op jit(solution)/shard_map/all_to_all | solution.py:110
  246.0 2.1 reshape.144
  248.0 2.0 fusion.36
  (55 shorter events, 8.6 us)
Async XLA Ops:
  6.5 124.4 %copy-start = (bf16[1280,3,320]{0,2,1:T(8,128)(2,1)S(1)}, bf16[1280,3,320]{0,2,1:T(8,128)(2,1)}, u32[]{:S(2)}) copy-start(bf16[1280,3,320]{0,2,1:T(8,128)(2,1)} %param.16) | copy-start | bytes 7372804
  6.5 121.1 %all-gather.3.cloned.1.call-start = ((), (), s32[]{:S(2)}) async-start(), calls=%async_computation.4 | async-start | bytes 3276800 | tf_op jit(solution)/shard_map/all_gather | solution.py:94
  7.4 7.6 %copy-start.8 = (s32[1,128]{1,0:T(1,128)S(1)}, s32[1,128]{1,0:T(1,128)}, u32[]{:S(2)}) copy-start(s32[1,128]{1,0:T(1,128)} %param.12) | copy-start | bytes 1540
  17.5 1.2 copy-start.1
  21.7 7.4 %copy-start.9 = (s32[128,1]{0,1:T(1,128)S(1)}, s32[128,1]{0,1:T(1,128)}, u32[]{:S(2)}) copy-start(s32[128,1]{0,1:T(1,128)} %param.13) | copy-start | bytes 1540
  21.7 7.6 %copy-start.4 = (bf16[128,1280]{1,0:T(8,128)(2,1)S(1)}, bf16[128,1280]{1,0:T(8,128)(2,1)}, u32[]{:S(2)}) copy-start(bf16[128,1280]{1,0:T(8,128)(2,1)} %param.11) | copy-start | bytes 983044
  29.1 60.2 %copy-start.2 = (bf16[128,1280]{1,0:T(8,128)(2,1)}, bf16[128,1280]{1,0:T(8,128)(2,1)S(1)}, u32[]{:S(2)}) copy-start(bf16[128,1280]{1,0:T(8,128)(2,1)S(1)} %scatter_custom_fusion) | copy-start | bytes 983044
  30.5 70.4 %copy-start.6 = (bf16[3,320]{1,0:T(4,128)(2,1)S(1)}, bf16[3,320]{1,0:T(4,128)(2,1)}, u32[]{:S(2)}) copy-start(bf16[3,320]{1,0:T(4,128)(2,1)} %param.17) | copy-start | bytes 5764
  30.5 70.4 %copy-start.5 = (s32[1,128]{1,0:T(1,128)S(1)}, s32[1,128]{1,0:T(1,128)}, u32[]{:S(2)}) copy-start(s32[1,128]{1,0:T(1,128)} %param.14) | copy-start | bytes 1540
  88.4 42.5 %copy-start.7 = (f32[1280]{0:T(1024)S(1)}, f32[1280]{0:T(1024)}, u32[]{:S(2)}) copy-start(f32[1280]{0:T(1024)} %param.15) | copy-start | bytes 15364
  90.3 25.3 %all-to-all-start = ((bf16[128,1,2]{2,1,0:T(2,128)(2,1)}), bf16[128,1,2]{2,1,0:T(2,128)(2,1)S(1)}, u32[]{:S(2)}, u32[]{:S(2)}) async-start(bf16[128,1,2]{2,1,0:T(2,128)(2,1)} %all_to_all.33), calls=%async_computation | async-start | bytes 131072 | tf_op jit(solution)/shard_map/all_to_all | solution.py:90
  190.4 57.6 %copy-start.3 = (bf16[128,1280]{1,0:T(8,128)(2,1)S(1)}, bf16[128,1280]{1,0:T(8,128)(2,1)}, u32[]{:S(2)}) copy-start(bf16[128,1280]{1,0:T(8,128)(2,1)} %copy-done.2) | copy-start | bytes 983044
Sparse Core Ops, SparseCore 0:
  89.5 38.1 all-gather.2

commit v2 on v1

v2 whole, which is shorter than its diff:
```python
import functools

import jax
import jax.numpy as jnp
from jax import lax
from jax.experimental import pallas as pl
from jax.experimental.pallas import tpu as pltpu
from jax.sharding import PartitionSpec as P

HD = 80
NORM_EPS = 1e-06
NZ, NX, NC, NY = 16, 4, 2, 4
NP = NX * NC
ROWS, WIDTH = 128, 1280
LANES = 128
HEADS_HERE = 4
PART = HEADS_HERE * LANES
PAIR = 2 * HEADS_HERE * HD
DEAD = 1024.0
SCALE = HD ** (-0.5)
LOG2E = 1.4426950408889634
MESH = pl.DeviceIdType.MESH
BF, F32, I32 = jnp.bfloat16, jnp.float32, jnp.int32


def hop(i):
    return (8 + (2 * (i % 2) - 1) * ((i + 1) // 2)) % NZ


def hop_of(i):
    return (8 + (2 * (i & 1) - 1) * ((i + 1) >> 1)) & (NZ - 1)


def iota(shape, axis):
    return lax.broadcasted_iota(I32, shape, axis)


def dot(a, b):
    return jnp.dot(a, b, preferred_element_type=F32)


def dot_nt(a, b):
    return lax.dot_general(a, b, (((1,), (1,)), ((), ())), preferred_element_type=F32)


def onehot(mask):
    return jnp.where(mask, 1.0, 0.0).astype(BF)


def rows16(index):
    return pl.ds(pl.multiple_of(index * 16, 16), 16)


def kernel(
    qkv_ref, state_ref, order_ref, owner_ref, request_ref, gain_ref, w_hbm, bias_ref, out_ref,
    moved, outgoing, plane_in, z_out, group, w_ref, asks, queries, keys, values, mixed,
    pieces, plane_back, z_back, final,
    w_sem, p_send, p_recv, z_send, z_recv, y_send, yl_recv, yr_recv, yx_recv,
    b_send, b_recv, r_send, r_recv,
):
    sec, sp, dev = (lax.axis_index(a) for a in ("sec", "sp", "dev"))
    x, z = dev // NZ, dev % NZ
    cx = sec * NX + x
    right, left = (sp + 1) % NY, (sp + 3) % NY

    load_w = pltpu.make_async_copy(w_hbm, w_ref, w_sem)
    load_w.start()

    def plane_id(to_cx, to_y):
        return (to_cx // NX, to_y, (to_cx % NX) * NZ + z)

    def z_id(to_z):
        return (sec, sp, x * NZ + to_z)

    barrier = pltpu.get_barrier_semaphore()

    def greet_plane(k, carry):
        pl.semaphore_signal(
            barrier, inc=1, device_id=plane_id((cx + k // NY) % NP, (sp + k % NY) % NY), device_id_type=MESH
        )
        return carry

    def greet_z(k, carry):
        pl.semaphore_signal(barrier, inc=1, device_id=z_id((z + k) % NZ), device_id_type=MESH)
        return carry

    lax.fori_loop(1, NP * NY, greet_plane, 0)
    lax.fori_loop(1, NZ, greet_z, 0)

    owner_cols = jnp.broadcast_to(owner_ref[...].astype(F32), (ROWS, ROWS))
    owner_rows = jnp.transpose(owner_cols)
    row_i, col_i = iota((ROWS, ROWS), 0), iota((ROWS, ROWS), 1)
    same = owner_cols == owner_rows
    rank_row = jnp.sum(jnp.where(same & (row_i < col_i), 1.0, 0.0), axis=0, keepdims=True)
    rank_col = jnp.sum(jnp.where(same & (col_i < row_i), 1.0, 0.0), axis=1, keepdims=True)

    order = jnp.broadcast_to(order_ref[...], (ROWS, ROWS))
    in_second = jnp.sum(jnp.where((order == row_i) & (col_i >= 64), 1.0, 0.0), axis=1, keepdims=True)
    second_cols = jnp.broadcast_to(in_second, (ROWS, ROWS))
    same_window = second_cols == jnp.transpose(second_cols)

    def window_half(half, carry):
        base = half * 640
        tiles = [jnp.zeros((ROWS, LANES), F32) for _ in range(5)]
        for head in range(8):
            low, high = head * HD, head * HD + HD
            first, last = low // LANES, (high + LANES - 1) // LANES
            span = (last - first) * LANES
            columns = pl.ds(pl.multiple_of(base + first * LANES, LANES), span)
            lane = iota((ROWS, span), 1) + first * LANES
            mine = (lane >= low) & (lane < high)
            q = qkv_ref[0, :, columns]
            q = jnp.where(mine, q.astype(F32), 0.0).astype(BF)
            scores = dot_nt(q, qkv_ref[1, :, columns])
            scores = jnp.where(same_window, scores * SCALE, -1e30)
            top = jnp.max(scores, axis=1, keepdims=True)
            expo = jnp.exp(scores - top)
            weights = (expo / jnp.sum(expo, axis=1, keepdims=True)).astype(BF)
            got = dot(weights, qkv_ref[2, :, columns])
            got = jnp.where(mine, got, 0.0)
            for t in range(first, last):
                tiles[t] = tiles[t] + got[:, (t - first) * LANES : (t - first + 1) * LANES]
        for t in range(5):
            columns = pl.ds(pl.multiple_of(base + t * LANES, LANES), LANES)
            window_out = tiles[t].astype(BF).astype(F32)
            moved[:, columns] = (state_ref[:, columns].astype(F32) + window_out).astype(BF)
        return carry

    lax.fori_loop(0, 2, window_half, 0)

    slot_i = iota((256, ROWS), 0)
    index = ((slot_i >> 7) << 3) + ((slot_i >> 1) & 7)
    to_owner = ((slot_i >> 4) & 7) * NZ + ((z + hop_of(index)) & (NZ - 1))
    chosen = (owner_rows[0:1] == to_owner.astype(F32)) & (rank_row == (slot_i & 1).astype(F32))
    picker = onehot(chosen)
    taken = jnp.max(jnp.where(chosen, 1.0, 0.0), axis=1, keepdims=True)
    outgoing[:, 0:LANES] = jnp.where(taken > 0.5, dot(picker, moved[:, 0:LANES]), DEAD).astype(BF)
    outgoing[:, LANES:] = dot(picker, moved[:, LANES:]).astype(BF)

    pl.semaphore_wait(barrier, NP * NY - 1 + NZ - 1)

    for half in range(2):

        def send_plane(k, carry):
            to = (cx + k) % NP
            pltpu.make_async_remote_copy(
                src_ref=outgoing.at[rows16(half * NP + to)], dst_ref=plane_in.at[rows16(half * NP + cx)],
                send_sem=p_send, recv_sem=p_recv.at[half], device_id=plane_id(to, sp), device_id_type=MESH,
            ).start()
            return carry

        lax.fori_loop(1, NP, send_plane, 0)
        plane_in[rows16(half * NP + cx)] = outgoing[rows16(half * NP + cx)]

    def local(ref, rows, send_sem, recv_sem):
        part = ref.at[pl.ds(0, rows)]
        return pltpu.make_async_remote_copy(
            src_ref=part, dst_ref=part, send_sem=send_sem, recv_sem=recv_sem,
            device_id=(sec, right, dev), device_id_type=MESH,
        )

    r, c = iota((ROWS, ROWS), 0), iota((ROWS, ROWS), 1)
    by_hop = onehot(c == (r & 7) * 16 + (r >> 4) * 2 + ((r >> 3) & 1))

    def send_z(i, carry):
        pltpu.make_async_remote_copy(
            src_ref=z_out.at[rows16(i)], dst_ref=group.at[rows16(i * NY + sp)],
            send_sem=z_send, recv_sem=z_recv.at[i], device_id=z_id((z + hop(i)) % NZ), device_id_type=MESH,
        ).start()
        return carry

    for half in range(2):
        local(plane_in, 7 * 16, p_send, p_recv.at[half]).wait_recv()
        z_out[half * 128 : half * 128 + 128] = dot(by_hop, plane_in[half * 128 : half * 128 + 128]).astype(BF)
        lax.fori_loop(half * 8, 8 if half == 0 else 15, send_z, 0)
    group[rows16(15 * NY + sp)] = z_out[240:256]

    r, c = iota((1024, LANES), 0), iota((1024, LANES), 1)
    source = (r & 7) * NZ + ((z - hop_of(r >> 6)) & (NZ - 1))
    lane_request = onehot(jnp.broadcast_to(request_ref[...], (LANES, LANES)) == row_i - HD)
    asks[...] = dot_nt(onehot(c == source), lane_request).astype(BF)
    load_w.wait()

    r, c = iota((256, 256), 0), iota((256, 256), 1)
    by_source = onehot(c == (r & 3) * 64 + ((r >> 2) & 3) * 16 + ((r >> 4) & 1) * 8 + (r >> 5))

    def send_y(i, from_y, to_y, recv_sem):
        part = group.at[rows16(i * NY + from_y)]
        pltpu.make_async_remote_copy(
            src_ref=part, dst_ref=part, send_sem=y_send, recv_sem=recv_sem,
            device_id=(sec, to_y, dev), device_id_type=MESH,
        ).start()

    def wait_one(recv_sem):
        local(group, 16, y_send, recv_sem).wait_recv()

    def relay(i):
        if i % 2 == 0:
            wait_one(yl_recv.at[i])
            send_y(i, left, right, yx_recv.at[i])
        else:
            wait_one(yr_recv.at[i])
            send_y(i, right, left, yx_recv.at[i])

    def project(k):
        for i in range(4 * k, 4 * k + 4):
            wait_one(yr_recv.at[i] if i % 2 == 0 else yl_recv.at[i])
            wait_one(yx_recv.at[i])
        rows = slice(256 * k, 256 * k + 256)
        raw = group[rows].astype(F32)
        live = raw[:, 0:1] < DEAD / 2
        mean_sq = jnp.mean(raw * raw, axis=1, keepdims=True)
        normed = (raw * lax.rsqrt(mean_sq + NORM_EPS) * gain_ref[...]).astype(BF)
        ask = asks[rows].astype(F32)
        lane = iota((256, LANES), 1)
        shut = jnp.where((lane >= HD) & (lane < HD + 8) & ~((ask > 0.5) & live), -1e30, 0.0)
        ones = jnp.where(lane == HD, 1.0, 0.0)
        for part, extra in enumerate((ask, shut, ones)):
            extra = jnp.concatenate([extra, extra], axis=1)
            for pair in range(2):
                columns = slice(part * PART + pair * 256, part * PART + pair * 256 + 256)
                here = slice(pair * 256, pair * 256 + 256)
                got = (dot(normed, w_ref[:, columns]) + (bias_ref[:, columns] + extra)).astype(BF)
                if part == 0:
                    got = dot(by_source, got).astype(BF)
                    for n in range(NP):
                        queries[n * 128 + k * 32 : n * 128 + k * 32 + 32, here] = got[n * 32 : n * 32 + 32]
                elif part == 1:
                    keys[rows, here] = got
                else:
                    values[rows, here] = got

    for i in range(16):
        if i < 15:
            local(group, 16, z_send, z_recv.at[i]).wait_recv()
        send_y(i, sp, right, yl_recv.at[i])
        send_y(i, sp, left, yr_recv.at[i])
        if i >= 1:
            relay(i - 1)
        if i >= 6 and i % 4 == 2:
            project(i // 4 - 1)
    relay(15)
    project(3)

    r, c = iota((PART, PAIR), 0), iota((PART, PAIR), 1)
    spot = (r >> 7) * HD + (r & 127)
    real = (r & 127) < HD
    place = [onehot(real & (c == spot + slot * HEADS_HERE * HD)) for slot in range(2)]
    r, c = iota((64, 256), 0), iota((64, 256), 1)
    gather_slots = onehot((c & 127) == ((r >> 2) & 3) * 32 + (c >> 7) * 16 + (r >> 4) * 4 + (r & 3))

    def attend(t):
        blocks = [pl.ds(pl.multiple_of(((cx + 2 * t + n) % NP) * 128, 128), 128) for n in range(2)]
        for head in range(HEADS_HERE):
            here = slice(head * LANES, head * LANES + LANES)
            q = jnp.concatenate([queries[b, here] for b in blocks], axis=0)
            scores = dot_nt(q, keys[:, here])
            top = jnp.max(scores, axis=1, keepdims=True)
            weights = jnp.exp2((scores - top) * (SCALE * LOG2E)).astype(BF)
            got = dot(weights, values[:, here])
            mixed[:, here] = (got / got[:, HD : HD + 1]).astype(BF)
        placed = [dot(mixed[...], p).astype(BF) for p in place]
        for n in range(2):
            e = 2 * t + n
            both = jnp.concatenate([p[n * 128 : n * 128 + 128] for p in placed], axis=0)
            pieces[e * 64 : e * 64 + 64] = dot(gather_slots, both).astype(BF)
            to = (cx + e) % NP
            for dy in range(NY):
                y = (sp + dy) % NY
                if e == 0 and dy == 0:
                    plane_back[rows16(sp)] = pieces[rows16(sp)]
                    continue
                pltpu.make_async_remote_copy(
                    src_ref=pieces.at[rows16(e * NY + y)], dst_ref=plane_back.at[rows16(e * NY + sp)],
                    send_sem=b_send, recv_sem=b_recv.at[e // 4], device_id=plane_id(to, y), device_id_type=MESH,
                ).start()

    r, c = iota((256, 256), 0), iota((256, 256), 1)
    by_hop_back = onehot(c == (r & 15) * 16 + (r >> 4))

    def give_back(half):
        local(plane_back, (15 + half) * 16, b_send, b_recv.at[half]).wait_recv()
        z_back[half * 256 : half * 256 + 256] = dot(by_hop_back, plane_back[half * 256 : half * 256 + 256]).astype(BF)

        def send_back(i, carry):
            rows = rows16(half * 16 + i)
            pltpu.make_async_remote_copy(
                src_ref=z_back.at[rows], dst_ref=final.at[rows], send_sem=r_send, recv_sem=r_recv,
                device_id=z_id((z + NZ - hop(i)) % NZ), device_id_type=MESH,
            ).start()
            return carry

        lax.fori_loop(0, 15, send_back, 0)
        final[half * 256 + 240 : half * 256 + 256] = z_back[half * 256 + 240 : half * 256 + 256]

    attend(0)
    attend(1)
    attend(2)
    give_back(0)
    attend(3)
    give_back(1)

    f = iota((1, 512), 1)
    from_cx = (cx - ((f >> 8) * 4 + ((f >> 2) & 3))) & (NP - 1)
    from_owner = (from_cx * NZ + ((z + hop_of((f >> 4) & 15)) & (NZ - 1))).astype(F32)
    mine = jnp.where(owner_cols[:, 0:1] == from_owner, 1.0, 0.0)
    local(final, 480, r_send, r_recv).wait_recv()
    lane = iota((ROWS, PAIR), 1)
    for pair in range(2):
        found = []
        for n in range(2):
            pick = jnp.where((f & 3) == 2 * pair + n, mine, 0.0).astype(BF)
            got = dot(pick, final[...])
            turned = pltpu.roll(got, PAIR // 2, 1)
            found.append(jnp.where(rank_col == float(n), got, turned))
        back = jnp.where(lane < PAIR // 2, found[0], found[1])
        columns = slice(pair * PAIR, pair * PAIR + PAIR)
        out_ref[:, columns] = (moved[:, columns].astype(F32) + back).astype(BF)

    local(outgoing, 14 * 16, p_send, p_recv.at[0]).wait_send()
    local(z_out, 15 * 16, z_send, z_recv.at[0]).wait_send()
    local(group, 48 * 16, y_send, yx_recv.at[0]).wait_send()
    local(pieces, 31 * 16, b_send, b_recv.at[0]).wait_send()
    local(z_back, 30 * 16, r_send, r_recv).wait_send()


def shards(
    patch_qkv, patch_state, window_index, patch_owner, source_request, norm_gain, w_qkv, b_qkv
):
    qkv = jnp.transpose(patch_qkv, (1, 0, 2))
    w = w_qkv.reshape(WIDTH, 3 * HEADS_HERE, HD)
    w = jnp.pad(w, ((0, 0), (0, 0), (0, LANES - HD))).reshape(WIDTH, 3 * PART)
    bias = jnp.pad(b_qkv.astype(F32).reshape(3 * HEADS_HERE, HD), ((0, 0), (0, LANES - HD))).reshape(1, 3 * PART)
    vmem = pl.BlockSpec(memory_space=pltpu.VMEM)
    dma = pltpu.SemaphoreType.DMA
    return pl.pallas_call(
        kernel,
        out_shape=jax.ShapeDtypeStruct((ROWS, WIDTH), BF),
        in_specs=[vmem] * 6 + [pl.BlockSpec(memory_space=pl.ANY), vmem],
        out_specs=vmem,
        scratch_shapes=[
            pltpu.VMEM((ROWS, WIDTH), BF),
            pltpu.VMEM((256, WIDTH), BF),
            pltpu.VMEM((256, WIDTH), BF),
            pltpu.VMEM((256, WIDTH), BF),
            pltpu.VMEM((1024, WIDTH), BF),
            pltpu.VMEM((WIDTH, 3 * PART), BF),
            pltpu.VMEM((1024, LANES), BF),
            pltpu.VMEM((1024, PART), BF),
            pltpu.VMEM((1024, PART), BF),
            pltpu.VMEM((1024, PART), BF),
            pltpu.VMEM((256, PART), BF),
            pltpu.VMEM((512, PAIR), BF),
            pltpu.VMEM((512, PAIR), BF),
            pltpu.VMEM((512, PAIR), BF),
            pltpu.VMEM((512, PAIR), BF),
            dma, dma, dma((2,)), dma, dma((16,)), dma, dma((16,)), dma((16,)), dma((16,)),
            dma, dma((2,)), dma, dma,
        ],
        compiler_params=pltpu.CompilerParams(
            collective_id=0, has_side_effects=True, vmem_limit_bytes=48 * 1024 * 1024
        ),
    )(qkv, patch_state, window_index, patch_owner, source_request, norm_gain.reshape(1, WIDTH), w, bias)


def solution(mesh):
    in_specs = (
        P(("sec", "sp", "dev"), None, None),
        P(("sec", "sp", "dev"), None),
        P(("sec", "sp", "dev"), None),
        P(("sec", "sp", "dev"), None),
        P(("sec", "dev"), None),
        P(),
        P(None, None, "sp"),
        P(None, "sp"),
    )
    out_specs = P(("sec", "sp", "dev"), None)
    return jax.shard_map(shards, mesh=mesh, in_specs=in_specs, out_specs=out_specs, check_vma=False)
```

time: 259 us -> 137 us (0.53)
  blocking collectives: 131 us -> 0 us
  Pallas kernels: 0 us -> 123 us
  matrix products: 41.1 us -> 0 us
  local copies, waits for them, and re-layouts: 31.6 us -> 13.4 us
  waiting for transfers between devices: 17.3 us -> 0 us
  between operations: 13.6 us -> 0.1 us
  starting transfers between devices: 10.6 us -> 0 us
  other arithmetic: 7.6 us -> 0.01 us
  loops' own time: 4.18 us -> 0 us
    pallas_call x0 -> x1, Pallas kernels: none -> 123 us  [shards(): pl.pallas_call(kernel, out_shape=jax.ShapeDtypeStruct((ROWS, WIDTH), BF),...]
    all_to_all x3 -> x0, blocking collectives: 122 us -> none  [the longest x1 55.9 us: shards(): lax.all_to_all(outgoing, ('sec', 'dev'), split_axis=0, concat_axis=0, til...]
    dot_general x7 -> x0, matrix products: 23.9 us -> none  [the longest x2 11.4 us: one_block(): jnp.einsum('hqk,khd->qhd', weights, values_all, preferred_element_type=jn...]
    sub x3 -> x0, matrix products: 17.2 us -> none  [softmax_rows(): expo_vals = jnp.exp(scores - row_max)]
    all_to_all x1 -> x0, waiting for transfers between devices: 14.4 us -> none  [shards(): lax.all_to_all(filled, ('sec', 'dev'), split_axis=0, concat_axis=0, tiled...]
    all_to_all x1 -> x0, starting transfers between devices: 10.6 us -> none  [shards(): lax.all_to_all(filled, ('sec', 'dev'), split_axis=0, concat_axis=0, tiled...]
    all_gather x1 -> x0, blocking collectives: 8.95 us -> none  [shards(): lax.all_gather(arrived, 'sp', axis=1, tiled=True)]
    gather x2 -> x0, local copies, waits for them, and re-layouts: 7.11 us -> none  [window_attend(): ordered = jnp.take(qkv_rows, order_ids, axis=0)]
  transfers between devices with their start and end apart: 2 -> 0, of which waited for: 2 -> 0; matrix products, arithmetic and copies ran while one was open for 0% -> 0% of each run, Pallas kernels for 0% -> 0%
where the time goes in v2:
time: 137 us
  Pallas kernels  123 us (90%)
  local copies, waits for them, and re-layouts  13.4 us (10%)
    pallas_call x1, Pallas kernels, shards(): pl.pallas_call(kernel, out_shape=jax.ShapeDtypeStruct((ROWS, WIDTH), BF),...  123 us
    reshape x1, local copies, waits for them, and re-layouts, shards(): w = jnp.pad(w, ((0, 0), (0, 0), (0, LANES - HD))).reshape(WIDTH, 3 * PART)  6.37 us
    pad x1, local copies, waits for them, and re-layouts, shards(): w = jnp.pad(w, ((0, 0), (0, 0), (0, LANES - HD))).reshape(WIDTH, 3 * PART)  3.92 us
    unnamed x19, local copies, waits for them, and re-layouts  2.99 us

profile of v2, /device:TPU:1, one launch (start us, length us, event | category | flops | bytes accessed | tf_op | source)
XLA Modules:
  0.0 136.9 jit_solution(1143323833935104302)
XLA Ops:
  0.0 3.9 %pad.9 = bf16[1280,12,128]{0,2,1:T(8,128)(2,1)} pad(bf16[1280,12,80]{0,2,1:T(8,128)(2,1)} %bitcast.12, bf16[]{:T(256)} %constant.4.clone.1), padding=0_0x0_0x0_48 | pad | bytes 6389762 | tf_op jit(solution)/shard_map/jit(_pad)/pad | solution.py:332
  3.9 0.0 copy-start.7
  3.9 0.0 copy-start.6
  3.9 0.0 copy-start.5
  3.9 0.0 copy-start.1
  3.9 0.0 copy-start.2
  3.9 0.0 copy-start.3
  4.0 0.0 copy-start.4
  4.0 6.4 %copy.12.w_hbm = bf16[1280,1536]{1,0:T(8,128)(2,1)} copy(bf16[1280,1536]{0,1:T(8,128)(2,1)} %bitcast.11) | data formatting | bytes 7864320 | tf_op jit(solution)/shard_map/reshape | solution.py:332
  10.3 0.0 copy-done.7
  10.3 0.1 copy.11.owner_ref
  10.5 0.0 copy-done.6
  10.5 0.1 reshape.21
  10.6 0.0 copy-done.5
  10.6 0.0 copy-done.1
  10.6 0.0 copy-done.2
  10.6 0.0 copy-done.3
  10.6 0.0 copy-done.4
  10.6 0.0 copy-start
  10.6 2.1 %copy-done = bf16[1280,1536]{1,0:T(8,128)(2,1)S(1)} copy-done((bf16[1280,1536]{1,0:T(8,128)(2,1)S(1)}, bf16[1280,1536]{1,0:T(8,128)(2,1)}, u32[]{:S(2)}) %copy-start) | copy-done | bytes 3932184
  12.7 123.4 %shard_map.82 = bf16[128,1280]{1,0:T(8,128)(2,1)S(1)} custom-call(bf16[3,128,1280]{2,1,0:T(8,128)(2,1)S(1)} %bitcast.9, bf16[128,1280]{1,0:T(8,128)(2,1)S(1)} %copy-done.2, s32[1,128]{1,0:T(1,128)S(1)} %copy-done.3, s32[128,1]{1,0:T(8,128)S(1)} %copy.11.owner_ref, s32[1,128]{1,0:T(1,128)S(1)} %copy-done.4, f32[1,1280]{1,0:T(1,128)S(1)} %reshape.18.gain_ref, ...), custom_call_target="tpu_custom_call" | custom-call | tf_op jit(solution)/shard_map/pallas_call | solution.py:336
  136.2 0.7 copy.17
  (3 shorter events, 0.0 us)
Async XLA Ops:
  3.9 6.4 %copy-start.7 = (s32[128,1]{0,1:T(1,128)S(1)}, s32[128,1]{0,1:T(1,128)}, u32[]{:S(2)}) copy-start(s32[128,1]{0,1:T(1,128)} %param.11) | copy-start | bytes 1540
  3.9 6.5 %copy-start.6 = (bf16[3,320]{1,0:T(4,128)(2,1)S(1)}, bf16[3,320]{1,0:T(4,128)(2,1)}, u32[]{:S(2)}) copy-start(bf16[3,320]{1,0:T(4,128)(2,1)} %param.15) | copy-start | bytes 5764
  3.9 6.6 %copy-start.5 = (f32[1280]{0:T(1024)S(1)}, f32[1280]{0:T(1024)}, u32[]{:S(2)}) copy-start(f32[1280]{0:T(1024)} %param.13) | copy-start | bytes 15364
  3.9 6.7 %copy-start.1 = (bf16[128,3,1280]{2,0,1:T(8,128)(2,1)S(1)}, bf16[128,3,1280]{2,0,1:T(8,128)(2,1)}, u32[]{:S(2)}) copy-start(bf16[128,3,1280]{2,0,1:T(8,128)(2,1)} %param.8) | copy-start | bytes 2949124
  3.9 6.7 %copy-start.2 = (bf16[128,1280]{1,0:T(8,128)(2,1)S(1)}, bf16[128,1280]{1,0:T(8,128)(2,1)}, u32[]{:S(2)}) copy-start(bf16[128,1280]{1,0:T(8,128)(2,1)} %state_ref.1) | copy-start | bytes 983044
  3.9 6.7 %copy-start.3 = (s32[1,128]{1,0:T(1,128)S(1)}, s32[1,128]{1,0:T(1,128)}, u32[]{:S(2)}) copy-start(s32[1,128]{1,0:T(1,128)} %order_ref.1) | copy-start | bytes 1540
  4.0 6.7 %copy-start.4 = (s32[1,128]{1,0:T(1,128)S(1)}, s32[1,128]{1,0:T(1,128)}, u32[]{:S(2)}) copy-start(s32[1,128]{1,0:T(1,128)} %request_ref.1) | copy-start | bytes 1540
  10.6 2.1 %copy-start = (bf16[1280,1536]{1,0:T(8,128)(2,1)S(1)}, bf16[1280,1536]{1,0:T(8,128)(2,1)}, u32[]{:S(2)}) copy-start(bf16[1280,1536]{1,0:T(8,128)(2,1)} %copy.12.w_hbm) | copy-start | bytes 11796484

commit v3 on v2

v3 whole, which is shorter than its diff:
```python
import functools

import jax
import jax.numpy as jnp
from jax import lax
from jax.experimental import pallas as pl
from jax.experimental.pallas import tpu as pltpu
from jax.sharding import PartitionSpec as P

HD = 80
NORM_EPS = 1e-06
NZ, NX, NC, NY = 16, 4, 2, 4
NP = NX * NC
ROWS, WIDTH = 128, 1280
LANES = 128
HEADS_HERE = 4
PART = HEADS_HERE * LANES
PAIR = 2 * HEADS_HERE * HD
DEAD = 1024.0
SCALE = HD ** (-0.5)
LOG2E = 1.4426950408889634
MESH = pl.DeviceIdType.MESH
BF, F32, I32 = jnp.bfloat16, jnp.float32, jnp.int32


def hop(i):
    return ((2 * (i % 2) - 1) * ((i + 1) // 2)) % NZ


def hop_of(i):
    return ((2 * (i & 1) - 1) * ((i + 1) >> 1)) & (NZ - 1)


def iota(shape, axis):
    return lax.broadcasted_iota(I32, shape, axis)


def dot(a, b):
    return jnp.dot(a, b, preferred_element_type=F32)


def dot_nt(a, b):
    return lax.dot_general(a, b, (((1,), (1,)), ((), ())), preferred_element_type=F32)


def onehot(mask):
    return jnp.where(mask, 1.0, 0.0).astype(BF)


def rows16(index):
    return pl.ds(pl.multiple_of(index * 16, 16), 16)


def kernel(
    qkv_hbm, state_hbm, order_ref, owner_ref, request_ref, gain_ref, w_hbm, b_ref, out_ref,
    qkv_ref, state_ref, bias_ref,
    moved, outgoing, near_in, near_out, far_in, far_out, group, w_ref, asks, queries, keys, values, mixed,
    pieces, plane_back, z_back, back_in, back_out, final,
    q_sem, w_sem, n_send, nz_recv, nx_recv, f_send, fx_recv, fz_recv, y_send, yl_recv, yr_recv, yx_recv,
    b_send, b_recv, fb_recv, r_send, r_recv, rb_recv,
):
    sec, sp, dev = (lax.axis_index(a) for a in ("sec", "sp", "dev"))
    x, z = dev // NZ, dev % NZ
    cx = sec * NX + x
    right, left = (sp + 1) % NY, (sp + 3) % NY

    load_qkv = pltpu.make_async_copy(qkv_hbm, qkv_ref, q_sem.at[0])
    load_state = pltpu.make_async_copy(state_hbm, state_ref, q_sem.at[1])
    load_w = [
        pltpu.make_async_copy(
            w_hbm.at[part, pl.ds(head * HD, HD)], w_ref.at[pl.ds(part * PART + head * LANES, HD)],
            w_sem.at[part * HEADS_HERE + head],
        )
        for part in range(3)
        for head in range(HEADS_HERE)
    ]
    load_qkv.start()
    load_state.start()
    for load in load_w:
        load.start()

    def plane_id(to_cx, to_y):
        return (to_cx // NX, to_y, (to_cx % NX) * NZ + z)

    def z_id(to_z):
        return (sec, sp, x * NZ + to_z)

    gain = gain_ref[...].reshape(1, WIDTH)
    barrier = pltpu.get_barrier_semaphore()

    def greet_plane(k, carry):
        pl.semaphore_signal(
            barrier, inc=1, device_id=plane_id((cx + k // NY) % NP, (sp + k % NY) % NY), device_id_type=MESH
        )
        return carry

    def greet_z(k, carry):
        pl.semaphore_signal(barrier, inc=1, device_id=z_id((z + k) % NZ), device_id_type=MESH)
        return carry

    lax.fori_loop(1, NP * NY, greet_plane, 0)
    lax.fori_loop(1, NZ, greet_z, 0)

    owner_rows = jnp.broadcast_to(owner_ref[...].astype(F32), (ROWS, ROWS))
    owner_cols = jnp.transpose(owner_rows)
    row_i, col_i = iota((ROWS, ROWS), 0), iota((ROWS, ROWS), 1)
    same = owner_cols == owner_rows
    rank_row = jnp.sum(jnp.where(same & (row_i < col_i), 1.0, 0.0), axis=0, keepdims=True)
    rank_col = jnp.sum(jnp.where(same & (col_i < row_i), 1.0, 0.0), axis=1, keepdims=True)

    order = jnp.broadcast_to(order_ref[...], (ROWS, ROWS))
    in_second = jnp.sum(jnp.where((order == row_i) & (col_i >= 64), 1.0, 0.0), axis=1, keepdims=True)
    second_cols = jnp.broadcast_to(in_second, (ROWS, ROWS))
    same_window = second_cols == jnp.transpose(second_cols)

    def window_half(half, carry):
        base = half * 640
        tiles = [jnp.zeros((ROWS, LANES), F32) for _ in range(5)]
        for head in range(8):
            low, high = head * HD, head * HD + HD
            first, last = low // LANES, (high + LANES - 1) // LANES
            span = (last - first) * LANES
            columns = pl.ds(pl.multiple_of(base + first * LANES, LANES), span)
            lane = iota((ROWS, span), 1) + first * LANES
            mine = (lane >= low) & (lane < high)
            q = qkv_ref[0, :, columns]
            q = jnp.where(mine, q.astype(F32), 0.0).astype(BF)
            scores = dot_nt(q, qkv_ref[1, :, columns])
            scores = jnp.where(same_window, scores * SCALE, -1e30)
            top = jnp.max(scores, axis=1, keepdims=True)
            expo = jnp.exp(scores - top)
            weights = (expo / jnp.sum(expo, axis=1, keepdims=True)).astype(BF)
            got = dot(weights, qkv_ref[2, :, columns])
            got = jnp.where(mine, got, 0.0)
            for t in range(first, last):
                tiles[t] = tiles[t] + got[:, (t - first) * LANES : (t - first + 1) * LANES]
        for t in range(5):
            columns = pl.ds(pl.multiple_of(base + t * LANES, LANES), LANES)
            window_out = tiles[t].astype(BF).astype(F32)
            moved[:, columns] = (state_ref[:, columns].astype(F32) + window_out).astype(BF)
        return carry

    load_qkv.wait()
    load_state.wait()
    lax.fori_loop(0, 2, window_half, 0)

    slot_i = iota((256, ROWS), 0)
    high, low = (slot_i >> 4) & 7, (slot_i >> 1) & 7
    far = slot_i >= 128
    to_z = (z + hop_of(jnp.where(far, 8 + low, high))) & (NZ - 1)
    to_owner = jnp.where(far, high, low) * NZ + to_z
    chosen = (owner_rows[0:1] == to_owner.astype(F32)) & (rank_row == (slot_i & 1).astype(F32))
    picker = onehot(chosen)
    taken = jnp.max(jnp.where(chosen, 1.0, 0.0), axis=1, keepdims=True)
    outgoing[:, 0:LANES] = jnp.where(taken > 0.5, dot(picker, moved[:, 0:LANES]), DEAD).astype(BF)
    outgoing[:, LANES:] = dot(picker, moved[:, LANES:]).astype(BF)

    pl.semaphore_wait(barrier, NP * NY - 1 + NZ - 1)

    def start(src, dst, send_sem, recv_sem, to):
        pltpu.make_async_remote_copy(
            src_ref=src, dst_ref=dst, send_sem=send_sem, recv_sem=recv_sem, device_id=to, device_id_type=MESH
        ).start()

    def waiter(ref, rows, send_sem, recv_sem):
        part = ref.at[pl.ds(0, rows)]
        return pltpu.make_async_remote_copy(
            src_ref=part, dst_ref=part, send_sem=send_sem, recv_sem=recv_sem,
            device_id=(sec, right, dev), device_id_type=MESH,
        )

    def near_z(i, carry):
        rows = rows16(i)
        start(outgoing.at[rows], near_in.at[rows], n_send.at[0], nz_recv, z_id((z + hop(i)) % NZ))
        return carry

    def far_plane(k, carry):
        to = (cx + k) % NP
        start(outgoing.at[rows16(8 + to)], far_in.at[rows16(cx)], f_send.at[0], fx_recv, plane_id(to, sp))
        return carry

    lax.fori_loop(1, NP, far_plane, 0)
    lax.fori_loop(1, 8, near_z, 0)
    far_in[rows16(cx)] = outgoing[rows16(8 + cx)]
    near_in[0:16] = outgoing[0:16]

    r, c = iota((ROWS, ROWS), 0), iota((ROWS, ROWS), 1)
    swap = onehot(c == (r & 7) * 16 + (r >> 4) * 2 + ((r >> 3) & 1))

    waiter(far_in, 7 * 16, f_send.at[0], fx_recv).wait_recv()
    far_out[...] = dot(swap, far_in[...]).astype(BF)

    def far_z(n, carry):
        to = z_id((z + hop(8 + n)) % NZ)
        start(far_out.at[rows16(n)], group.at[rows16(32 + n * NY + sp)], f_send.at[1], fz_recv.at[n], to)
        return carry

    lax.fori_loop(0, 8, far_z, 0)

    waiter(near_in, 7 * 16, n_send.at[0], nz_recv).wait_recv()
    near_out[...] = dot(swap, near_in[...]).astype(BF)

    def near_plane(k, carry):
        to = (cx + k) % NP
        start(near_out.at[rows16(to)], group.at[rows16(cx * NY + sp)], n_send.at[1], nx_recv.at[k], plane_id(to, sp))
        return carry

    lax.fori_loop(1, NP, near_plane, 0)
    group[rows16(cx * NY + sp)] = near_out[rows16(cx)]

    r, c = iota((1024, LANES), 0), iota((1024, LANES), 1)
    high, low = (r >> 6) & 7, r & 7
    source = jnp.where(r < 512, high, low) * NZ + ((z - hop_of(jnp.where(r < 512, low, 8 + high))) & (NZ - 1))
    lane_request = onehot(jnp.broadcast_to(request_ref[...], (LANES, LANES)) == row_i - HD)
    asks[...] = dot_nt(onehot(c == source), lane_request).astype(BF)
    r, c = iota((HEADS_HERE * HD, PART), 0), iota((HEADS_HERE * HD, PART), 1)
    spread = onehot(((c & 127) < HD) & (r == (c >> 7) * HD + (c & 127)))
    for part in range(3):
        bias_ref[:, part * PART : part * PART + PART] = dot(b_ref[part : part + 1], spread)
        for head in range(HEADS_HERE):
            unused = part * PART + head * LANES + HD
            w_ref[unused : unused + LANES - HD] = jnp.zeros((LANES - HD, WIDTH), BF)
    for load in load_w:
        load.wait()

    r, c = iota((256, 256), 0), iota((256, 256), 1)
    by_source = onehot(c == (r & 3) * 64 + ((r >> 2) & 3) * 16 + ((r >> 4) & 1) * 8 + (r >> 5))

    def block(n, y):
        return rows16(((cx + NP - n) % NP if n < 8 else n) * NY + y)

    def send_y(n, from_y, to_y, recv_sem):
        part = group.at[block(n, from_y)]
        start(part, part, y_send, recv_sem, (sec, to_y, dev))

    def wait_one(recv_sem):
        waiter(group, 16, y_send, recv_sem).wait_recv()

    def forward(n):
        if n > 0:
            wait_one(nx_recv.at[n] if n < 8 else fz_recv.at[n - 8])
        send_y(n, sp, right, yl_recv.at[n])
        send_y(n, sp, left, yr_recv.at[n])

    def relay(n):
        if n % 2 == 0:
            wait_one(yl_recv.at[n])
            send_y(n, left, right, yx_recv.at[n])
        else:
            wait_one(yr_recv.at[n])
            send_y(n, right, left, yx_recv.at[n])

    def settle(n):
        wait_one(yr_recv.at[n] if n % 2 == 0 else yl_recv.at[n])
        wait_one(yx_recv.at[n])

    def project(k):
        rows = slice(256 * k, 256 * k + 256)
        raw = group[rows].astype(F32)
        live = raw[:, 0:1] < DEAD / 2
        mean_sq = jnp.mean(raw * raw, axis=1, keepdims=True)
        normed = (raw * lax.rsqrt(mean_sq + NORM_EPS) * gain).astype(BF)
        ask = asks[rows].astype(F32)
        lane = iota((256, LANES), 1)
        shut = jnp.where((lane >= HD) & (lane < HD + 8) & ~((ask > 0.5) & live), -1e30, 0.0)
        ones = jnp.where(lane == HD, 1.0, 0.0)
        for part, extra in enumerate((ask, shut, ones)):
            extra = jnp.concatenate([extra, extra], axis=1)
            for pair in range(2):
                columns = slice(part * PART + pair * 256, part * PART + pair * 256 + 256)
                here = slice(pair * 256, pair * 256 + 256)
                got = (dot_nt(normed, w_ref[columns]) + (bias_ref[:, columns] + extra)).astype(BF)
                if part == 0:
                    if k < 2:
                        for n in range(4):
                            to = (4 * k + n) * 128
                            queries[to : to + 64, here] = got[n * 64 : n * 64 + 64]
                        continue
                    got = dot(by_source, got).astype(BF)
                    for n in range(NP):
                        to = n * 128 + k * 32
                        queries[to : to + 32, here] = got[n * 32 : n * 32 + 32]
                elif part == 1:
                    keys[rows, here] = got
                else:
                    values[rows, here] = got

    for n in range(16):
        forward(n)
        if n >= 2:
            relay(n - 2)
        if n == 10:
            for m in range(8):
                settle(m)
            project(0)
        if n == 11:
            project(1)
        if n == 14:
            for m in range(8, 12):
                settle(m)
            project(2)
    relay(14)
    relay(15)
    for m in range(12, 16):
        settle(m)
    project(3)

    r, c = iota((PART, PAIR), 0), iota((PART, PAIR), 1)
    spot = (r >> 7) * HD + (r & 127)
    real = (r & 127) < HD
    place = [onehot(real & (c == spot + slot * HEADS_HERE * HD)) for slot in range(2)]
    r, c = iota((64, 256), 0), iota((64, 256), 1)
    slot, y, i = c >> 7, r >> 4, r & 15
    near_row, far_row = y * 16 + slot * 8 + i, 64 + ((i - 8) >> 2) * 32 + slot * 16 + y * 4 + (i & 3)
    gather_slots = onehot((c & 127) == jnp.where(i < 8, near_row, far_row))

    def attend(t):
        blocks = [pl.ds(pl.multiple_of(((cx + 2 * t + n) % NP) * 128, 128), 128) for n in range(2)]
        for head in range(HEADS_HERE):
            here = slice(head * LANES, head * LANES + LANES)
            q = jnp.concatenate([queries[b, here] for b in blocks], axis=0)
            scores = dot_nt(q, keys[:, here])
            top = jnp.max(scores, axis=1, keepdims=True)
            weights = jnp.exp2((scores - top) * (SCALE * LOG2E)).astype(BF)
            got = dot(weights, values[:, here])
            mixed[:, here] = (got / got[:, HD : HD + 1]).astype(BF)
        placed = [dot(mixed[...], p).astype(BF) for p in place]
        for n in range(2):
            e = 2 * t + n
            both = jnp.concatenate([p[n * 128 : n * 128 + 128] for p in placed], axis=0)
            pieces[e * 64 : e * 64 + 64] = dot(gather_slots, both).astype(BF)
            if t < 2:
                continue
            for dy in range(NY):
                y = (sp + dy) % NY
                start(
                    pieces.at[rows16(e * NY + y)], plane_back.at[rows16((e - 4) * NY + sp)],
                    b_send.at[0], b_recv, plane_id((cx + e) % NP, y),
                )

    r, c = iota((256, 256), 0), iota((256, 256), 1)
    turn = onehot(c == (r & 15) * 16 + (r >> 4))

    attend(0)
    attend(1)
    z_back[0:256] = dot(turn, pieces[0:256]).astype(BF)

    def first_z(n, carry):
        i = 15 - n
        start(z_back.at[rows16(i)], back_in.at[rows16(i)], r_send.at[0], rb_recv, z_id((z + NZ - hop(i)) % NZ))
        return carry

    lax.fori_loop(0, 15, first_z, 0)
    back_in[0:16] = z_back[0:16]
    attend(2)
    attend(3)
    waiter(plane_back, 16 * 16, b_send.at[0], b_recv).wait_recv()
    z_back[256:512] = dot(turn, plane_back[...]).astype(BF)

    def second_z(n, carry):
        rows = rows16(31 - n)
        start(z_back.at[rows], final.at[rows], r_send.at[1], r_recv, z_id((z + NZ - hop(15 - n)) % NZ))
        return carry

    lax.fori_loop(0, 15, second_z, 0)
    final[256:272] = z_back[256:272]
    waiter(back_in, 15 * 16, r_send.at[0], rb_recv).wait_recv()
    back_out[...] = dot(turn, back_in[...]).astype(BF)

    def first_plane(k, carry):
        e, y = k // NY, (sp + k % NY) % NY
        to = plane_id((cx + e) % NP, y)
        start(back_out.at[rows16(e * NY + y)], final.at[rows16(e * NY + sp)], b_send.at[1], fb_recv, to)
        return carry

    lax.fori_loop(1, 16, first_plane, 0)
    final[rows16(sp)] = back_out[rows16(sp)]

    f = iota((1, 512), 1)
    e = jnp.where(f < 256, f >> 6, 4 + ((f >> 2) & 3))
    by_y = jnp.where(f < 256, f >> 4, f) & 3
    from_z = (z + hop_of(jnp.where(f < 256, f, f >> 4) & 15)) & (NZ - 1)
    from_owner = (((cx - e) & (NP - 1)) * NZ + from_z).astype(F32)
    mine = jnp.where(owner_cols[:, 0:1] == from_owner, 1.0, 0.0)
    waiter(final, 15 * 16, r_send.at[1], r_recv).wait_recv()
    waiter(final, 15 * 16, b_send.at[1], fb_recv).wait_recv()
    lane = iota((ROWS, PAIR), 1)
    for pair in range(2):
        found = []
        for n in range(2):
            pick = jnp.where(by_y == 2 * pair + n, mine, 0.0).astype(BF)
            got = dot(pick, final[...])
            turned = pltpu.roll(got, PAIR // 2, 1)
            found.append(jnp.where(rank_col == float(n), got, turned))
        back = jnp.where(lane < PAIR // 2, found[0], found[1])
        columns = slice(pair * PAIR, pair * PAIR + PAIR)
        out_ref[:, columns] = (moved[:, columns].astype(F32) + back).astype(BF)

    waiter(outgoing, 7 * 16, n_send.at[0], nz_recv).wait_send()
    waiter(outgoing, 7 * 16, f_send.at[0], fx_recv).wait_send()
    waiter(outgoing, 7 * 16, n_send.at[1], nz_recv).wait_send()
    waiter(outgoing, 8 * 16, f_send.at[1], fx_recv).wait_send()
    waiter(group, 48 * 16, y_send, yx_recv.at[0]).wait_send()
    waiter(pieces, 16 * 16, b_send.at[0], b_recv).wait_send()
    waiter(pieces, 15 * 16, b_send.at[1], b_recv).wait_send()
    waiter(z_back, 15 * 16, r_send.at[0], r_recv).wait_send()
    waiter(z_back, 15 * 16, r_send.at[1], r_recv).wait_send()


def shards(
    patch_qkv, patch_state, window_index, patch_owner, source_request, norm_gain, w_qkv, b_qkv
):
    vmem = pl.BlockSpec(memory_space=pltpu.VMEM)
    hbm = pl.BlockSpec(memory_space=pl.ANY)
    dma = pltpu.SemaphoreType.DMA
    return pl.pallas_call(
        kernel,
        out_shape=jax.ShapeDtypeStruct((ROWS, WIDTH), BF),
        in_specs=[hbm] * 2 + [vmem] * 4 + [hbm, vmem],
        out_specs=vmem,
        scratch_shapes=[
            pltpu.VMEM((3, ROWS, WIDTH), BF),
            pltpu.VMEM((ROWS, WIDTH), BF),
            pltpu.VMEM((1, 3 * PART), F32),
            pltpu.VMEM((ROWS, WIDTH), BF),
            pltpu.VMEM((256, WIDTH), BF),
            pltpu.VMEM((128, WIDTH), BF),
            pltpu.VMEM((128, WIDTH), BF),
            pltpu.VMEM((128, WIDTH), BF),
            pltpu.VMEM((128, WIDTH), BF),
            pltpu.VMEM((1024, WIDTH), BF),
            pltpu.VMEM((3 * PART, WIDTH), BF),
            pltpu.VMEM((1024, LANES), BF),
            pltpu.VMEM((1024, PART), BF),
            pltpu.VMEM((1024, PART), BF),
            pltpu.VMEM((1024, PART), BF),
            pltpu.VMEM((256, PART), BF),
            pltpu.VMEM((512, PAIR), BF),
            pltpu.VMEM((256, PAIR), BF),
            pltpu.VMEM((512, PAIR), BF),
            pltpu.VMEM((256, PAIR), BF),
            pltpu.VMEM((256, PAIR), BF),
            pltpu.VMEM((512, PAIR), BF),
            dma((2,)), dma((12,)), dma((2,)), dma, dma((8,)), dma((2,)), dma, dma((8,)),
            dma, dma((16,)), dma((16,)), dma((16,)),
            dma((2,)), dma, dma, dma((2,)), dma, dma,
        ],
        compiler_params=pltpu.CompilerParams(
            collective_id=0, has_side_effects=True, vmem_limit_bytes=60 * 1024 * 1024
        ),
    )(
        jnp.transpose(patch_qkv, (1, 0, 2)), patch_state, window_index, patch_owner.reshape(1, ROWS), source_request,
        norm_gain, jnp.transpose(w_qkv, (1, 2, 0)), b_qkv,
    )


def solution(mesh):
    in_specs = (
        P(("sec", "sp", "dev"), None, None),
        P(("sec", "sp", "dev"), None),
        P(("sec", "sp", "dev"), None),
        P(("sec", "sp", "dev"), None),
        P(("sec", "dev"), None),
        P(),
        P(None, None, "sp"),
        P(None, "sp"),
    )
    out_specs = P(("sec", "sp", "dev"), None)
    return jax.shard_map(shards, mesh=mesh, in_specs=in_specs, out_specs=out_specs, check_vma=False)
```

time: 137 us -> 108 us (0.79)
  Pallas kernels: 123 us -> 106 us
  local copies, waits for them, and re-layouts: 13.4 us -> 1.72 us
    pallas_call x1, Pallas kernels: 123 us -> 106 us  [shards(): pl.pallas_call(kernel, out_shape=jax.ShapeDtypeStruct((ROWS, WIDTH), BF),...]
    reshape x3 -> x0, local copies, waits for them, and re-layouts: 6.47 us -> none  [the longest x1 6.37 us: shards(): w = jnp.pad(w, ((0, 0), (0, 0), (0, LANES - HD))).reshape(WIDTH, 3 * PART)]
    pad x1 -> x0, local copies, waits for them, and re-layouts: 3.92 us -> none  [shards(): w = jnp.pad(w, ((0, 0), (0, 0), (0, LANES - HD))).reshape(WIDTH, 3 * PART)]
    unnamed x19 -> x1, local copies, waits for them, and re-layouts: 2.99 us -> 1.72 us
where the time goes in v3:
time: 108 us
  Pallas kernels  106 us (98%)
  local copies, waits for them, and re-layouts  1.72 us (2%)
    pallas_call x1, Pallas kernels, shards(): pl.pallas_call(kernel, out_shape=jax.ShapeDtypeStruct((ROWS, WIDTH), BF),...  106 us

profile of v3, /device:TPU:1, one launch (start us, length us, event | category | flops | bytes accessed | tf_op | source)
XLA Modules:
  0.0 107.6 jit_solution(4069045791129719216)
XLA Ops:
  0.0 105.9 %shard_map.82 = bf16[128,1280]{1,0:T(8,128)(2,1)} custom-call(bf16[3,128,1280]{2,1,0:T(8,128)(2,1)} %bitcast.4, bf16[128,1280]{1,0:T(8,128)(2,1)} %state_hbm.1, s32[1,128]{1,0:T(1,128)} %order_ref.1, s32[1,128]{1,0:T(1,128)} %bitcast.5, s32[1,128]{1,0:T(1,128)} %request_ref.1, f32[1280]{0:T(1024)} %gain_ref.1, bf16[3,320,1280]{2,1,0:T(8,128)(2,1)} %bitcast.3, ...), custom_call_target="tpu_custom_call" | custom-call | tf_op jit(solution)/shard_map/pallas_call | solution.py:416
  105.9 1.7 %copy.10 = bf16[128,1280]{1,0:T(8,128)(2,1)} copy(bf16[128,1280]{1,0:T(8,128)(2,1)} %shard_map.82) | data formatting | bytes 655360

commit v4 on v3

--- a/solution.py
+++ b/solution.py
@@ -179,8 +179,8 @@
         start(outgoing.at[rows16(8 + to)], far_in.at[rows16(cx)], f_send.at[0], fx_recv, plane_id(to, sp))
         return carry
 
+    lax.fori_loop(1, 8, near_z, 0)
     lax.fori_loop(1, NP, far_plane, 0)
-    lax.fori_loop(1, 8, near_z, 0)
     far_in[rows16(cx)] = outgoing[rows16(8 + cx)]
     near_in[0:16] = outgoing[0:16]
 
@@ -289,18 +289,17 @@
         forward(n)
         if n >= 2:
             relay(n - 2)
-        if n == 10:
+        if n == 14:
             for m in range(8):
                 settle(m)
             project(0)
-        if n == 11:
+        if n == 15:
             project(1)
-        if n == 14:
-            for m in range(8, 12):
-                settle(m)
-            project(2)
     relay(14)
     relay(15)
+    for m in range(8, 12):
+        settle(m)
+    project(2)
     for m in range(12, 16):
         settle(m)
     project(3)

time: 108 us -> 102 us (0.944)
  Pallas kernels: 106 us -> 99.9 us
    pallas_call x1, Pallas kernels: 106 us -> 99.9 us  [shards(): pl.pallas_call(kernel, out_shape=jax.ShapeDtypeStruct((ROWS, WIDTH), BF),...]
where the time goes in v4:
time: 102 us
  Pallas kernels  99.9 us (98%)
  local copies, waits for them, and re-layouts  1.72 us (2%)
    pallas_call x1, Pallas kernels, shards(): pl.pallas_call(kernel, out_shape=jax.ShapeDtypeStruct((ROWS, WIDTH), BF),...  99.9 us

profile of v4, /device:TPU:1, one launch (start us, length us, event | category | flops | bytes accessed | tf_op | source)
XLA Modules:
  0.0 101.6 jit_solution(3442892615642016749)
XLA Ops:
  0.0 99.9 %shard_map.82 = bf16[128,1280]{1,0:T(8,128)(2,1)} custom-call(bf16[3,128,1280]{2,1,0:T(8,128)(2,1)} %bitcast.4, bf16[128,1280]{1,0:T(8,128)(2,1)} %state_hbm.1, s32[1,128]{1,0:T(1,128)} %order_ref.1, s32[1,128]{1,0:T(1,128)} %bitcast.5, s32[1,128]{1,0:T(1,128)} %request_ref.1, f32[1280]{0:T(1024)} %gain_ref.1, bf16[3,320,1280]{2,1,0:T(8,128)(2,1)} %bitcast.3, ...), custom_call_target="tpu_custom_call" | custom-call | tf_op jit(solution)/shard_map/pallas_call | solution.py:415
  99.9 1.7 %copy.10 = bf16[128,1280]{1,0:T(8,128)(2,1)} copy(bf16[128,1280]{1,0:T(8,128)(2,1)} %shard_map.82) | data formatting | bytes 655360
